TPU v7x, 256 devices: a whole 4x4x8 slice. The times are simulated.
256 devices in a mesh: rows: 32 (over x, y, core), height: 8 (over z).
Axes of the slice: x: 4, y: 4, z: 8, core: 2. Of those that a mesh axis runs over, the one named last changes fastest.
Arguments:
- snapshots: float32 [64, 256, 128, 128], P(None, 'rows', 'height'), may hold values from -200 to 200
- material: int32 [256, 128, 128], P('rows', 'height'), may hold values from 0 to 2
Outputs:
- basis: float32 [64, 256, 128, 128], P(None, 'rows', 'height')
- applied: float32 [64, 256, 128, 128], P(None, 'rows', 'height')
- reduced: float32 [64, 64], replicated
- low_factor: float32 [64, 64], replicated
All inputs are finite; a program needn't handle non-finite values.
Results may differ from a plain program's by a relative error of at most 0.00014.
Values sent between devices are 32-bit elements; how exact they have to be, the bound alone decides.
A program may use at most 64 MiB of HBM per device.

v0:
```python
import functools

import jax
import jax.numpy as jnp
from jax import lax
from jax.experimental import pallas as pl
from jax.experimental.pallas import tpu as pltpu
from jax.sharding import PartitionSpec as P

CONDUCT_TABLE = (0.5, 2.0, 1.0)
COUPLE_TABLE = (0.3, 0.1, 0.6)
MESH = pl.DeviceIdType.MESH
F32 = jnp.float32
BF16 = jnp.bfloat16
M = 64
NXL, NZL, NY = 8, 16, 128
LANES = NZL * NY
ROWS, HEIGHT = 32, 8
CELLS = 4194304


def lookup(material, table):
    return jnp.where(material == 0, table[0], jnp.where(material == 1, table[1], table[2])).astype(F32)


def split3(f):
    h = f.astype(BF16)
    r = f - h.astype(F32)
    m = r.astype(BF16)
    return h, m, (r - m.astype(F32)).astype(BF16)


def tree_sum(vals):
    while len(vals) > 1:
        vals = [vals[i] + vals[i + 1] if i + 1 < len(vals) else vals[i] for i in range(0, len(vals), 2)]
    return vals[0]


def zsl(z):
    return slice(z * NY, (z + 1) * NY)


def pack(g):
    return jnp.concatenate([g[0:32], g[32:64]], axis=1)


def unpack(g):
    return jnp.concatenate([g[:, 0:64], g[:, 64:128]], axis=0)


def nt_dot(a, b):
    return lax.dot_general(a, b, (((1,), (1,)), ((), ())), preferred_element_type=F32)


def first_kernel(
    snap, mat_in, f3, i3, w_out, pt_out,
    mat, fld, hz_lo, hz_hi, cond, faces, coef, acc, acc2,
    mine, from_c, xy_buf, z_buf, half, whole,
    load_sem, fx_send, fx_recv, ar_send, ar_recv,
):
    r = lax.axis_index("rows")
    z = lax.axis_index("height")
    xy, c = r // 2, r % 2
    up_r, dn_r = (r + 1) % ROWS, (r + ROWS - 1) % ROWS
    up_z, dn_z = (z + 1) % HEIGHT, (z + HEIGHT - 1) % HEIGHT
    partner = (xy * 2 + (1 - c), z)

    def remote(src, dst, ss, rs, dev):
        return pltpu.make_async_remote_copy(
            src_ref=src, dst_ref=dst, send_sem=ss, recv_sem=rs, device_id=dev, device_id_type=MESH
        )

    def drain(ref, sem):
        pltpu.make_async_copy(ref, ref, sem).wait()

    def load(x):
        for zz in range(NZL):
            pltpu.make_async_copy(
                snap.at[:, x, zz, :], fld.at[x + 1, :, zsl(zz)], load_sem.at[x]
            ).start()

    def load_body(i, carry):
        load(i)
        return carry

    pltpu.make_async_copy(mat_in, mat, load_sem.at[NXL]).start()
    load(0)
    load(NXL - 1)
    lax.fori_loop(1, NXL - 1, load_body, 0)

    bar = pltpu.get_barrier_semaphore()

    def greet(dev):
        pl.semaphore_signal(bar, inc=1, device_id=dev, device_id_type=MESH)

    greet((up_r, z))
    greet((dn_r, z))
    greet(partner)
    for k in range(1, 16):
        greet((((xy + k) % 16) * 2 + c, z))
    for k in range(1, HEIGHT):
        greet((r, (z + k) % HEIGHT))

    drain(mat, load_sem.at[NXL])
    cond[...] = lookup(mat[...], CONDUCT_TABLE)
    faces[0] = cond[NXL - 1]
    faces[1] = cond[0]
    faces[2, 0:8] = cond[:, NZL - 1, :]
    faces[3, 0:8] = cond[:, 0, :]
    acc[...] = jnp.zeros_like(acc)
    acc2[...] = jnp.zeros_like(acc2)

    pl.semaphore_wait(bar, 2 + 1 + 15 + 7)
    remote(faces.at[0], faces.at[4], fx_send.at[0], fx_recv.at[0], (up_r, z)).start()
    remote(faces.at[1], faces.at[5], fx_send.at[1], fx_recv.at[1], (dn_r, z)).start()
    remote(faces.at[2, 0:8], faces.at[6, 0:8], fx_send.at[2], fx_recv.at[2], (r, up_z)).start()
    remote(faces.at[3, 0:8], faces.at[7, 0:8], fx_send.at[3], fx_recv.at[3], (r, dn_z)).start()

    def gram_part(x):
        drain(fld.at[x + 1], load_sem.at[x])
        remote(fld.at[x + 1, :, zsl(NZL - 1)], hz_lo.at[x], fx_send.at[4], fx_recv.at[4], (r, up_z)).start()
        remote(fld.at[x + 1, :, zsl(0)], hz_hi.at[x], fx_send.at[5], fx_recv.at[5], (r, dn_z)).start()
        for zz in range(NZL):
            h, m, low = split3(fld[x + 1, :, zsl(zz)])
            f3[x, 0:64, zsl(zz)] = h
            f3[x, 64:128, zsl(zz)] = m
            f3[x, 128:192, zsl(zz)] = low
        acc[...] += nt_dot(f3[x, 0:128], f3[x])

    gram_part(0)
    remote(fld.at[1], fld.at[NXL + 1], fx_send.at[6], fx_recv.at[6], (dn_r, z)).start()
    gram_part(NXL - 1)
    remote(fld.at[NXL], fld.at[0], fx_send.at[7], fx_recv.at[7], (up_r, z)).start()

    def gram_body(x, carry):
        gram_part(x)
        return carry

    lax.fori_loop(1, NXL - 1, gram_body, 0)

    def sum_start(i, value):
        mine[i] = value
        remote(
            mine.at[i, pl.ds(pl.multiple_of((1 - c) * 16, 16), 16)], from_c.at[i],
            ar_send.at[4 * i], ar_recv.at[4 * i], partner,
        ).start()

    def sum_xy(i):
        drain(from_c.at[i], ar_recv.at[4 * i])
        half[i, 0] = mine[i, pl.ds(pl.multiple_of(c * 16, 16), 16), :] + from_c[i]
        for k in range(1, 16):
            remote(
                half.at[i, 0], xy_buf.at[i, xy], ar_send.at[4 * i + 1], ar_recv.at[4 * i + 1],
                (((xy + k) % 16) * 2 + c, z),
            ).start()
        xy_buf[i, xy] = half[i, 0]

    def sum_z(i):
        drain(xy_buf.at[i, 0:15], ar_recv.at[4 * i + 1])
        half[i, 1] = tree_sum([xy_buf[i, k] for k in range(16)])
        for k in range(1, HEIGHT):
            remote(
                half.at[i, 1], z_buf.at[i, z], ar_send.at[4 * i + 2], ar_recv.at[4 * i + 2],
                (r, (z + k) % HEIGHT),
            ).start()
        z_buf[i, z] = half[i, 1]

    def sum_c(i):
        drain(z_buf.at[i, 0:7], ar_recv.at[4 * i + 2])
        here = whole.at[i, pl.ds(pl.multiple_of(c * 16, 16), 16)]
        here[...] = tree_sum([z_buf[i, k] for k in range(HEIGHT)])
        remote(here, here, ar_send.at[4 * i + 3], ar_recv.at[4 * i + 3], partner).start()

    def sum_end(i):
        there = whole.at[i, pl.ds(pl.multiple_of((1 - c) * 16, 16), 16)]
        drain(there, ar_recv.at[4 * i + 3])
        return unpack(whole[i])

    a = acc[...]
    cross = a[0:64, 64:128] + a[0:64, 128:192]
    gram = (a[0:64, 0:64] + (cross + cross.T) + a[64:128, 64:128]) * (1.0 / CELLS)
    sum_start(0, pack(gram))
    sum_xy(0)

    for i in range(4):
        drain(faces.at[4 + i] if i < 2 else faces.at[4 + i, 0:8], fx_recv.at[i])
    row_id = lax.broadcasted_iota(jnp.int32, (NZL, NY), 0)
    lane_id = lax.broadcasted_iota(jnp.int32, (NZL, NY), 1)
    ok_lo_x = jnp.where(r > 0, 1.0, 0.0).astype(F32)
    ok_hi_x = jnp.where(r < ROWS - 1, 1.0, 0.0).astype(F32)
    ok_lo_z = jnp.where(z > 0, 1.0, 0.0).astype(F32)
    ok_hi_z = jnp.where(z < HEIGHT - 1, 1.0, 0.0).astype(F32)
    for x in range(NXL):
        cc = cond[x]
        couple = lookup(mat[x], COUPLE_TABLE)
        half_c = 0.5 * cc
        diag = couple
        if x == 0:
            lo = 0.5 * (cc + faces[4]) * ok_lo_x
            diag = diag + half_c * (1.0 - ok_lo_x)
        else:
            lo = 0.5 * (cc + cond[x - 1])
        if x == NXL - 1:
            hi = 0.5 * (cc + faces[5]) * ok_hi_x
            diag = diag + half_c * (1.0 - ok_hi_x)
        else:
            hi = 0.5 * (cc + cond[x + 1])
        below = jnp.concatenate([faces[6, x : x + 1], cc[0 : NZL - 1]], axis=0)
        above = jnp.concatenate([cc[1:NZL], faces[7, x : x + 1]], axis=0)
        mask_lo = jnp.where(row_id == 0, ok_lo_z, 1.0)
        mask_hi = jnp.where(row_id == NZL - 1, ok_hi_z, 1.0)
        zlo = 0.5 * (cc + below) * mask_lo
        zhi = 0.5 * (cc + above) * mask_hi
        diag = diag + half_c * ((1.0 - mask_lo) + (1.0 - mask_hi))
        nxt = pltpu.roll(cc, NY - 1, 1)
        ly = jnp.where(lane_id == NY - 1, 0.0, 0.5 * (cc + nxt))
        edge = jnp.where((lane_id == 0) | (lane_id == NY - 1), half_c, 0.0)
        coef[0, x] = diag + edge
        coef[1, x] = lo
        coef[2, x] = hi
        coef[3, x] = zlo
        coef[4, x] = zhi
        coef[5, x] = ly

    drain(hz_lo, fx_recv.at[4])
    drain(hz_hi, fx_recv.at[5])
    drain(fld.at[NXL + 1], fx_recv.at[6])
    drain(fld.at[0], fx_recv.at[7])

    def image_part(x, carry):
        for zz in range(NZL):
            v = fld[x + 1, :, zsl(zz)]

            def cf(i):
                return coef[i, x, zz : zz + 1, :]

            out = cf(0) * v
            out += cf(1) * (v - fld[x, :, zsl(zz)])
            out += cf(2) * (v - fld[x + 2, :, zsl(zz)])
            out += cf(3) * (v - (hz_lo[x] if zz == 0 else fld[x + 1, :, zsl(zz - 1)]))
            out += cf(4) * (v - (hz_hi[x] if zz == NZL - 1 else fld[x + 1, :, zsl(zz + 1)]))
            q = cf(5) * (v - pltpu.roll(v, NY - 1, 1))
            out += q - pltpu.roll(q, 1, 1)
            h, m, low = split3(out)
            i3[x, 0:64, zsl(zz)] = h
            i3[x, 64:128, zsl(zz)] = m
            i3[x, 128:192, zsl(zz)] = low
        acc2[...] += nt_dot(f3[x], i3[x])
        return carry

    lax.fori_loop(0, NXL, image_part, 0)
    sum_z(0)

    a = acc2[...]
    proj = (
        a[0:64, 0:64]
        + (a[0:64, 64:128] + a[64:128, 0:64])
        + (a[0:64, 128:192] + a[64:128, 64:128] + a[128:192, 0:64])
    ) * (1.0 / CELLS)
    sum_start(1, pack(proj))
    sum_xy(1)
    sum_c(0)
    g = sum_end(0)
    sum_z(1)

    ri = lax.broadcasted_iota(jnp.int32, (M, M), 0)
    ci = lax.broadcasted_iota(jnp.int32, (M, M), 1)
    rows = lax.broadcasted_iota(jnp.int32, (M, 2 * M), 0)
    w = jnp.concatenate([g, jnp.where(ri == ci, 1.0, 0.0).astype(F32)], axis=1)
    for j in range(M - 1):
        row = w[j : j + 1, :]
        mult = w[:, j : j + 1] * (1.0 / w[j : j + 1, j : j + 1])
        w = jnp.where(rows > j, w - mult * row, w)
    w_out[...] = w

    sum_c(1)
    pt_out[...] = sum_end(1)

    for i in range(4):
        drain(faces.at[4] if i < 2 else faces.at[4, 0:8], fx_send.at[i])
    drain(hz_lo, fx_send.at[4])
    drain(hz_hi, fx_send.at[5])
    drain(fld.at[0], fx_send.at[6])
    drain(fld.at[0], fx_send.at[7])
    for i in range(2):
        drain(from_c.at[i], ar_send.at[4 * i])
        drain(xy_buf.at[i, 0:15], ar_send.at[4 * i + 1])
        drain(z_buf.at[i, 0:7], ar_send.at[4 * i + 2])
        drain(from_c.at[i], ar_send.at[4 * i + 3])


def last_kernel(f3, i3, w_in, pt, basis, applied, reduced, low_factor, st, lst, sem):
    w = w_in[...]
    ri = lax.broadcasted_iota(jnp.int32, (M, M), 0)
    ci = lax.broadcasted_iota(jnp.int32, (M, M), 1)
    u = w[:, 0:M]
    d = jnp.sum(jnp.where(ri == ci, u, 0.0), axis=1, keepdims=True)
    rs = lax.rsqrt(d)
    linv = jnp.where(ci <= ri, w[:, M : 2 * M] * rs, 0.0)
    h, m, low = split3(linv)
    zero = jnp.zeros_like(h)
    lst[...] = jnp.concatenate(
        [
            jnp.concatenate([h, h, h], axis=1),
            jnp.concatenate([m, m, zero], axis=1),
            jnp.concatenate([low, zero, zero], axis=1),
        ],
        axis=0,
    )

    def part(x, carry):
        for i, (src, dst) in enumerate(((f3, basis), (i3, applied))):
            for col in range(0, LANES, 512):
                p = jnp.dot(lst[...], src[x, :, col : col + 512], preferred_element_type=F32)
                st[i, x, :, col : col + 512] = p[0:64] + (p[64:128] + p[128:192])
            for zz in range(NZL):
                pltpu.make_async_copy(st.at[i, x, :, zsl(zz)], dst.at[:, x, zz, :], sem).start()
        return carry

    lax.fori_loop(0, NXL, part, 0)
    low_factor[...] = jnp.where(ci >= ri, u * rs, 0.0).T
    hi = lax.Precision.HIGHEST
    t = jnp.dot(linv, pt[...], precision=hi, preferred_element_type=F32)
    reduced[...] = lax.dot_general(
        t, linv, (((1,), (1,)), ((), ())), precision=hi, preferred_element_type=F32
    )
    pltpu.make_async_copy(st, st, sem).wait()


def local(snapshots, material):
    any_ = pl.BlockSpec(memory_space=pl.ANY)
    vm = pl.BlockSpec(memory_space=pltpu.VMEM)
    dma, fbuf = pltpu.SemaphoreType.DMA, functools.partial(pltpu.VMEM, dtype=F32)
    wide = pltpu.VMEM((NXL, 192, LANES), BF16)
    f3, i3, w, pt = pl.pallas_call(
        first_kernel,
        out_shape=(
            wide,
            wide,
            jax.ShapeDtypeStruct((M, 2 * M), F32),
            jax.ShapeDtypeStruct((M, M), F32),
        ),
        in_specs=[any_, any_],
        out_specs=(vm, vm, vm, vm),
        scratch_shapes=[
            pltpu.VMEM((NXL, NZL, NY), jnp.int32),
            fbuf((NXL + 2, M, LANES)),
            fbuf((NXL, M, NY)),
            fbuf((NXL, M, NY)),
            fbuf((NXL, NZL, NY)),
            fbuf((8, NZL, NY)),
            fbuf((6, NXL, NZL, NY)),
            fbuf((128, 192)),
            fbuf((192, 192)),
            fbuf((2, 32, 128)),
            fbuf((2, 16, 128)),
            fbuf((2, 16, 16, 128)),
            fbuf((2, 8, 16, 128)),
            fbuf((2, 2, 16, 128)),
            fbuf((2, 32, 128)),
            dma((NXL + 1,)),
            dma((8,)),
            dma((8,)),
            dma((8,)),
            dma((8,)),
        ],
        compiler_params=pltpu.CompilerParams(
            collective_id=0, has_side_effects=True, vmem_limit_bytes=24 << 20
        ),
        name="gram_and_image",
    )(
        pltpu.with_memory_space_constraint(snapshots, pltpu.HBM),
        pltpu.with_memory_space_constraint(material, pltpu.HBM),
    )
    full = jax.ShapeDtypeStruct((M, NXL, NZL, NY), F32)
    small = jax.ShapeDtypeStruct((M, M), F32)
    return pl.pallas_call(
        last_kernel,
        out_shape=(full, full, small, small),
        in_specs=[vm, vm, vm, vm],
        out_specs=(any_, any_, vm, vm),
        scratch_shapes=[fbuf((2, NXL, M, LANES)), pltpu.VMEM((192, 192), BF16), dma],
        compiler_params=pltpu.CompilerParams(vmem_limit_bytes=24 << 20),
        name="apply_inverse",
    )(f3, i3, w, pt)


def solution(mesh):
    in_specs = (P(None, "rows", "height", None), P("rows", "height", None))
    out_specs = (P(None, "rows", "height", None), P(None, "rows", "height", None), P(), P())
    return jax.shard_map(local, mesh=mesh, in_specs=in_specs, out_specs=out_specs, check_vma=False)
```

profile of v0, /device:TPU:1, one launch (start us, length us, event | category | flops | bytes accessed | tf_op | source)
XLA Modules:
  0.0 51.9 jit_solution(344816471249497202)
XLA Ops:
  0.6 43.1 %gram_and_image.1 = (bf16[8,192,2048]{2,1,0:T(8,128)(2,1)S(1)}, bf16[8,192,2048]{2,1,0:T(8,128)(2,1)S(1)}, f32[64,128]{1,0:T(8,128)S(1)}, f32[64,64]{1,0:T(8,128)S(1)}) custom-call(f32[64,8,16,128]{3,2,1,0:T(8,128)} %snap.1, s32[8,16,128]{2,1,0:T(8,128)} %mat_in.1), custom_call_target="tpu_custom_call" | custom-call | tf_op jit(solution)/shard_map/gram_and_image/pallas_call | solution.py:335
  43.7 8.2 %apply_inverse.1 = (f32[64,8,16,128]{3,2,1,0:T(8,128)}, f32[64,8,16,128]{3,2,1,0:T(8,128)}, f32[64,64]{1,0:T(8,128)}, f32[64,64]{1,0:T(8,128)}) custom-call(bf16[8,192,2048]{2,1,0:T(8,128)(2,1)S(1)} %get-tuple-element.8.f3, bf16[8,192,2048]{2,1,0:T(8,128)(2,1)S(1)} %get-tuple-element.9.i3, f32[64,128]{1,0:T(8,128)S(1)} %get-tuple-element.10.w_in, ...), custom_call_target="tpu_custom_call" | custom-call | tf_op jit(solution)/shard_map/apply_inverse/pallas_call | solution.py:377
where the time goes:
time: 52 us; the launch traced here: 51.9 us
  Pallas kernels  51.3 us (99%)
  between operations  0.64 us (1%)
    pallas_call x1, Pallas kernels, local(): pl.pallas_call(first_kernel, out_shape=(wide, wide, jax.ShapeDtypeStruct(...  43.1 us
    pallas_call x1, Pallas kernels, local(): pl.pallas_call(last_kernel, out_shape=(full, full, small, small), in_spec...  8.18 us

commit v1 on v0

--- a/solution.py
+++ b/solution.py
@@ -17,6 +17,7 @@
 LANES = NZL * NY
 ROWS, HEIGHT = 32, 8
 CELLS = 4194304
+PARTS = (slice(0, 64),)
 
 
 def lookup(material, table):
@@ -52,10 +53,39 @@
     return lax.dot_general(a, b, (((1,), (1,)), ((), ())), preferred_element_type=F32)
 
 
+def eliminate(w):
+    blocks = [w[8 * k : 8 * k + 8] for k in range(8)]
+    rid = lax.broadcasted_iota(jnp.int32, (8, 2 * M), 0)
+
+    def over_lanes(v, j):
+        return jnp.broadcast_to(v[:, j : j + 1], (8, 2 * M))
+
+    def over_rows(v, s):
+        return jnp.broadcast_to(v[s : s + 1, :], (8, 2 * M))
+
+    for b in range(8):
+        full = upper = blocks[b]
+        cols = [over_lanes(full, 8 * b + s) for s in range(8)]
+        below = [[over_lanes(blocks[k], 8 * b + s) for s in range(8)] for k in range(b + 1, 8)]
+        for s in range(8):
+            inv = 1.0 / over_rows(cols[s], s)
+            here = rid == s
+            mult = cols[s] * inv
+            upper = jnp.where(here, full, upper)
+            full = jnp.where(here, full * inv, full - mult * over_rows(full, s))
+            for t in range(s + 1, 8):
+                cols[t] = jnp.where(here, cols[t] * inv, cols[t] - mult * over_rows(cols[t], s))
+        rows = [over_rows(full, s) for s in range(8)]
+        for k in range(b + 1, 8):
+            blocks[k] = blocks[k] - tree_sum([below[k - b - 1][s] * rows[s] for s in range(8)])
+        blocks[b] = upper
+    return jnp.concatenate(blocks, axis=0)
+
+
 def first_kernel(
-    snap, mat_in, f3, i3, w_out, pt_out,
-    mat, fld, hz_lo, hz_hi, cond, faces, coef, acc, acc2,
-    mine, from_c, xy_buf, z_buf, half, whole,
+    snap, mat_in, basis_v, applied_v, w_out, pt_out,
+    mat, fld, lay, f3, i3, hz_out, hz_lo, hz_hi, cond, faces, coef, acc, acc2,
+    mine, from_c, xy_buf, z_buf, half, whole, lst,
     load_sem, fx_send, fx_recv, ar_send, ar_recv,
 ):
     r = lax.axis_index("rows")
@@ -73,20 +103,12 @@
     def drain(ref, sem):
         pltpu.make_async_copy(ref, ref, sem).wait()
 
-    def load(x):
-        for zz in range(NZL):
-            pltpu.make_async_copy(
-                snap.at[:, x, zz, :], fld.at[x + 1, :, zsl(zz)], load_sem.at[x]
-            ).start()
-
-    def load_body(i, carry):
-        load(i)
-        return carry
+    def slab(x, zz):
+        return fld.at[x].reshape(M * NZL, NY)[pl.ds(zz, M, stride=NZL), :]
 
     pltpu.make_async_copy(mat_in, mat, load_sem.at[NXL]).start()
-    load(0)
-    load(NXL - 1)
-    lax.fori_loop(1, NXL - 1, load_body, 0)
+    for x in (0, NXL - 1, *range(1, NXL - 1)):
+        pltpu.make_async_copy(snap.at[:, x], fld.at[x], load_sem.at[x]).start()
 
     bar = pltpu.get_barrier_semaphore()
 
@@ -110,30 +132,43 @@
     acc[...] = jnp.zeros_like(acc)
     acc2[...] = jnp.zeros_like(acc2)
 
+    def gram_part(x):
+        for zz in range(NZL):
+            v = slab(x, zz)
+            lay[x + 1, :, zsl(zz)] = v
+            if zz == 0:
+                hz_out[0, x] = v
+            if zz == NZL - 1:
+                hz_out[1, x] = v
+            h, m, low = split3(v)
+            f3[x, 0:64, zsl(zz)] = h
+            f3[x, 64:128, zsl(zz)] = m
+            f3[x, 128:192, zsl(zz)] = low
+        acc[...] += nt_dot(f3[x, 0:128], f3[x])
+
+    def send_z(x):
+        remote(hz_out.at[1, x], hz_lo.at[x], fx_send.at[4], fx_recv.at[4], (r, up_z)).start()
+        remote(hz_out.at[0, x], hz_hi.at[x], fx_send.at[5], fx_recv.at[5], (r, dn_z)).start()
+
+    drain(fld.at[0], load_sem.at[0])
+    gram_part(0)
+    drain(fld.at[NXL - 1], load_sem.at[NXL - 1])
+
     pl.semaphore_wait(bar, 2 + 1 + 15 + 7)
     remote(faces.at[0], faces.at[4], fx_send.at[0], fx_recv.at[0], (up_r, z)).start()
     remote(faces.at[1], faces.at[5], fx_send.at[1], fx_recv.at[1], (dn_r, z)).start()
     remote(faces.at[2, 0:8], faces.at[6, 0:8], fx_send.at[2], fx_recv.at[2], (r, up_z)).start()
     remote(faces.at[3, 0:8], faces.at[7, 0:8], fx_send.at[3], fx_recv.at[3], (r, dn_z)).start()
-
-    def gram_part(x):
-        drain(fld.at[x + 1], load_sem.at[x])
-        remote(fld.at[x + 1, :, zsl(NZL - 1)], hz_lo.at[x], fx_send.at[4], fx_recv.at[4], (r, up_z)).start()
-        remote(fld.at[x + 1, :, zsl(0)], hz_hi.at[x], fx_send.at[5], fx_recv.at[5], (r, dn_z)).start()
-        for zz in range(NZL):
-            h, m, low = split3(fld[x + 1, :, zsl(zz)])
-            f3[x, 0:64, zsl(zz)] = h
-            f3[x, 64:128, zsl(zz)] = m
-            f3[x, 128:192, zsl(zz)] = low
-        acc[...] += nt_dot(f3[x, 0:128], f3[x])
-
-    gram_part(0)
-    remote(fld.at[1], fld.at[NXL + 1], fx_send.at[6], fx_recv.at[6], (dn_r, z)).start()
+    remote(lay.at[1], lay.at[NXL + 1], fx_send.at[6], fx_recv.at[6], (dn_r, z)).start()
+    send_z(0)
     gram_part(NXL - 1)
-    remote(fld.at[NXL], fld.at[0], fx_send.at[7], fx_recv.at[7], (up_r, z)).start()
+    remote(lay.at[NXL], lay.at[0], fx_send.at[7], fx_recv.at[7], (up_r, z)).start()
+    send_z(NXL - 1)
 
     def gram_body(x, carry):
+        drain(fld.at[x], load_sem.at[x])
         gram_part(x)
+        send_z(x)
         return carry
 
     lax.fori_loop(1, NXL - 1, gram_body, 0)
@@ -180,7 +215,6 @@
     cross = a[0:64, 64:128] + a[0:64, 128:192]
     gram = (a[0:64, 0:64] + (cross + cross.T) + a[64:128, 64:128]) * (1.0 / CELLS)
     sum_start(0, pack(gram))
-    sum_xy(0)
 
     for i in range(4):
         drain(faces.at[4 + i] if i < 2 else faces.at[4 + i, 0:8], fx_recv.at[i])
@@ -222,34 +256,70 @@
         coef[4, x] = zhi
         coef[5, x] = ly
 
-    drain(hz_lo, fx_recv.at[4])
-    drain(hz_hi, fx_recv.at[5])
-    drain(fld.at[NXL + 1], fx_recv.at[6])
-    drain(fld.at[0], fx_recv.at[7])
-
-    def image_part(x, carry):
-        for zz in range(NZL):
-            v = fld[x + 1, :, zsl(zz)]
+    sum_xy(0)
+
+    def image(x, z0, z1, part):
+        def at(xx, zz):
+            return lay[xx, part, zsl(zz)]
+
+        v = at(x + 1, z0)
+        prev = hz_lo[x, part] if z0 == 0 else at(x + 1, z0 - 1)
+        flux = coef[3, x, z0 : z0 + 1, :] * (prev - v)
+        for zz in range(z0, z1):
+            nxt = hz_hi[x, part] if zz == NZL - 1 else at(x + 1, zz + 1)
 
             def cf(i):
                 return coef[i, x, zz : zz + 1, :]
 
-            out = cf(0) * v
-            out += cf(1) * (v - fld[x, :, zsl(zz)])
-            out += cf(2) * (v - fld[x + 2, :, zsl(zz)])
-            out += cf(3) * (v - (hz_lo[x] if zz == 0 else fld[x + 1, :, zsl(zz - 1)]))
-            out += cf(4) * (v - (hz_hi[x] if zz == NZL - 1 else fld[x + 1, :, zsl(zz + 1)]))
             q = cf(5) * (v - pltpu.roll(v, NY - 1, 1))
-            out += q - pltpu.roll(q, 1, 1)
-            h, m, low = split3(out)
-            i3[x, 0:64, zsl(zz)] = h
-            i3[x, 64:128, zsl(zz)] = m
-            i3[x, 128:192, zsl(zz)] = low
-        acc2[...] += nt_dot(f3[x], i3[x])
+            out = cf(0) * v - flux
+            out += cf(1) * (v - at(x, zz))
+            out += cf(2) * (v - at(x + 2, zz))
+            flux = cf(4) * (v - nxt)
+            out += flux + (q - pltpu.roll(q, 1, 1))
+            for k, piece in enumerate(split3(out)):
+                i3[x, k * M + part.start : k * M + part.stop, zsl(zz)] = piece
+            v = nxt
+
+    def images(x, z0, z1):
+        for part in PARTS:
+            image(x, z0, z1, part)
+
+    def inner_body(x, carry):
+        images(x, 1, NZL - 1)
+        cells = slice(NY, LANES - NY)
+        acc2[...] += nt_dot(f3[x, :, cells], i3[x, :, cells])
         return carry
 
-    lax.fori_loop(0, NXL, image_part, 0)
-    sum_z(0)
+    lax.fori_loop(1, NXL - 1, inner_body, 0)
+
+    def outer():
+        drain(hz_lo, fx_recv.at[4])
+        drain(hz_hi, fx_recv.at[5])
+        drain(lay.at[NXL + 1], fx_recv.at[6])
+        drain(lay.at[0], fx_recv.at[7])
+
+        def end_body(i, carry):
+            x = i * (NXL - 1)
+            images(x, 0, NZL)
+            acc2[...] += nt_dot(f3[x], i3[x])
+            return carry
+
+        def edge_body(x, carry):
+            images(x, 0, 1)
+            images(x, NZL - 1, NZL)
+
+            def both(ref):
+                return jnp.concatenate([ref[x, :, zsl(0)], ref[x, :, zsl(NZL - 1)]], axis=1)
+
+            acc2[...] += nt_dot(both(f3), both(i3))
+            return carry
+
+        lax.fori_loop(0, 2, end_body, 0)
+        sum_z(0)
+        lax.fori_loop(1, NXL - 1, edge_body, 0)
+
+    outer()
 
     a = acc2[...]
     proj = (
@@ -261,70 +331,68 @@
     sum_xy(1)
     sum_c(0)
     g = sum_end(0)
-    sum_z(1)
 
     ri = lax.broadcasted_iota(jnp.int32, (M, M), 0)
     ci = lax.broadcasted_iota(jnp.int32, (M, M), 1)
-    rows = lax.broadcasted_iota(jnp.int32, (M, 2 * M), 0)
-    w = jnp.concatenate([g, jnp.where(ri == ci, 1.0, 0.0).astype(F32)], axis=1)
-    for j in range(M - 1):
-        row = w[j : j + 1, :]
-        mult = w[:, j : j + 1] * (1.0 / w[j : j + 1, j : j + 1])
-        w = jnp.where(rows > j, w - mult * row, w)
-    w_out[...] = w
-
+    w = eliminate(jnp.concatenate([g, jnp.where(ri == ci, 1.0, 0.0).astype(F32)], axis=1))
+    u = w[:, 0:M]
+    d = jnp.sum(jnp.where(ri == ci, u, 0.0), axis=1, keepdims=True)
+    rs = lax.rsqrt(d)
+    linv = jnp.where(ci <= ri, w[:, M : 2 * M] * rs, 0.0)
+    upper = jnp.where(ci >= ri, u * rs, 0.0)
+    w_out[...] = jnp.concatenate([upper, linv], axis=1)
+    h, m, low = split3(linv)
+    zero = jnp.zeros_like(h)
+    lst[0:64] = jnp.concatenate([h, h, h, m], axis=1)
+    lst[64:128] = jnp.concatenate([low, m, zero, zero], axis=1)
+    sum_z(1)
+
+    step = 512
+
+    def inverse_body(x, carry):
+        for src, dst in ((f3, basis_v), (i3, applied_v)):
+            out = dst.at[x].reshape(M * NZL, NY)
+            for col in range(0, LANES, step):
+                cells = slice(col, col + step)
+                rhs = jnp.concatenate([src[x, :, cells], src[x, 0:64, cells]], axis=0)
+                p = jnp.dot(lst[...], rhs, preferred_element_type=F32)
+                p = p[0:64] + p[64:128]
+                for k in range(step // NY):
+                    out[pl.ds(col // NY + k, M, stride=NZL), :] = p[:, k * NY : (k + 1) * NY]
+        return carry
+
+    lax.fori_loop(0, NXL, inverse_body, 0)
     sum_c(1)
-    pt_out[...] = sum_end(1)
 
     for i in range(4):
         drain(faces.at[4] if i < 2 else faces.at[4, 0:8], fx_send.at[i])
     drain(hz_lo, fx_send.at[4])
     drain(hz_hi, fx_send.at[5])
-    drain(fld.at[0], fx_send.at[6])
-    drain(fld.at[0], fx_send.at[7])
+    drain(lay.at[0], fx_send.at[6])
+    drain(lay.at[0], fx_send.at[7])
     for i in range(2):
         drain(from_c.at[i], ar_send.at[4 * i])
         drain(xy_buf.at[i, 0:15], ar_send.at[4 * i + 1])
         drain(z_buf.at[i, 0:7], ar_send.at[4 * i + 2])
         drain(from_c.at[i], ar_send.at[4 * i + 3])
-
-
-def last_kernel(f3, i3, w_in, pt, basis, applied, reduced, low_factor, st, lst, sem):
+    pt_out[...] = sum_end(1)
+
+
+def last_kernel(basis_v, applied_v, w_in, pt, basis, applied, reduced, low_factor, sem):
+    for x in range(NXL):
+        pltpu.make_async_copy(basis_v.at[x], basis.at[:, x], sem).start()
+    for x in range(NXL):
+        pltpu.make_async_copy(applied_v.at[x], applied.at[:, x], sem).start()
     w = w_in[...]
-    ri = lax.broadcasted_iota(jnp.int32, (M, M), 0)
-    ci = lax.broadcasted_iota(jnp.int32, (M, M), 1)
-    u = w[:, 0:M]
-    d = jnp.sum(jnp.where(ri == ci, u, 0.0), axis=1, keepdims=True)
-    rs = lax.rsqrt(d)
-    linv = jnp.where(ci <= ri, w[:, M : 2 * M] * rs, 0.0)
-    h, m, low = split3(linv)
-    zero = jnp.zeros_like(h)
-    lst[...] = jnp.concatenate(
-        [
-            jnp.concatenate([h, h, h], axis=1),
-            jnp.concatenate([m, m, zero], axis=1),
-            jnp.concatenate([low, zero, zero], axis=1),
-        ],
-        axis=0,
-    )
-
-    def part(x, carry):
-        for i, (src, dst) in enumerate(((f3, basis), (i3, applied))):
-            for col in range(0, LANES, 512):
-                p = jnp.dot(lst[...], src[x, :, col : col + 512], preferred_element_type=F32)
-                st[i, x, :, col : col + 512] = p[0:64] + (p[64:128] + p[128:192])
-            for zz in range(NZL):
-                pltpu.make_async_copy(st.at[i, x, :, zsl(zz)], dst.at[:, x, zz, :], sem).start()
-        return carry
-
-    lax.fori_loop(0, NXL, part, 0)
-    low_factor[...] = jnp.where(ci >= ri, u * rs, 0.0).T
+    linv = w[:, M : 2 * M]
+    low_factor[...] = w[:, 0:M].T
     hi = lax.Precision.HIGHEST
     t = jnp.dot(linv, pt[...], precision=hi, preferred_element_type=F32)
     reduced[...] = lax.dot_general(
         t, linv, (((1,), (1,)), ((), ())), precision=hi, preferred_element_type=F32
     )
-    pltpu.make_async_copy(st, st, sem).wait()
+    pltpu.make_async_copy(basis_v, basis_v, sem).wait()
+    pltpu.make_async_copy(applied_v, applied_v, sem).wait()
 
 
 def local(snapshots, material):
@@ -332,19 +400,19 @@
     vm = pl.BlockSpec(memory_space=pltpu.VMEM)
     dma, fbuf = pltpu.SemaphoreType.DMA, functools.partial(pltpu.VMEM, dtype=F32)
     wide = pltpu.VMEM((NXL, 192, LANES), BF16)
-    f3, i3, w, pt = pl.pallas_call(
+    held = fbuf((NXL, M, NZL, NY))
+    basis_v, applied_v, w, pt = pl.pallas_call(
         first_kernel,
-        out_shape=(
-            wide,
-            wide,
-            jax.ShapeDtypeStruct((M, 2 * M), F32),
-            jax.ShapeDtypeStruct((M, M), F32),
-        ),
+        out_shape=(held, held, fbuf((M, 2 * M)), fbuf((M, M))),
         in_specs=[any_, any_],
         out_specs=(vm, vm, vm, vm),
         scratch_shapes=[
             pltpu.VMEM((NXL, NZL, NY), jnp.int32),
+            fbuf((NXL, M, NZL, NY)),
             fbuf((NXL + 2, M, LANES)),
+            wide,
+            wide,
+            fbuf((2, NXL, M, NY)),
             fbuf((NXL, M, NY)),
             fbuf((NXL, M, NY)),
             fbuf((NXL, NZL, NY)),
@@ -358,6 +426,7 @@
             fbuf((2, 8, 16, 128)),
             fbuf((2, 2, 16, 128)),
             fbuf((2, 32, 128)),
+            pltpu.VMEM((128, 256), BF16),
             dma((NXL + 1,)),
             dma((8,)),
             dma((8,)),
@@ -365,7 +434,7 @@
             dma((8,)),
         ],
         compiler_params=pltpu.CompilerParams(
-            collective_id=0, has_side_effects=True, vmem_limit_bytes=24 << 20
+            collective_id=0, has_side_effects=True, vmem_limit_bytes=32 << 20
         ),
         name="gram_and_image",
     )(
@@ -379,10 +448,10 @@
         out_shape=(full, full, small, small),
         in_specs=[vm, vm, vm, vm],
         out_specs=(any_, any_, vm, vm),
-        scratch_shapes=[fbuf((2, NXL, M, LANES)), pltpu.VMEM((192, 192), BF16), dma],
-        compiler_params=pltpu.CompilerParams(vmem_limit_bytes=24 << 20),
-        name="apply_inverse",
-    )(f3, i3, w, pt)
+        scratch_shapes=[dma],
+        compiler_params=pltpu.CompilerParams(vmem_limit_bytes=8 << 20),
+        name="write_results",
+    )(basis_v, applied_v, w, pt)
 
 
 def solution(mesh):

time: 52 us -> 42.5 us (0.82)
  Pallas kernels: 51.3 us -> 41.7 us
    pallas_call x1, Pallas kernels: 43.1 us -> 37.8 us  [local(): pl.pallas_call(first_kernel, out_shape=(held, held, fbuf((M, 2 * M)), fbu...]
    pallas_call x1, Pallas kernels: 8.18 us -> 3.91 us  [local(): pl.pallas_call(last_kernel, out_shape=(full, full, small, small), in_spec...]
where the time goes in v1:
time: 42.5 us; the launch traced here: 42.4 us
  Pallas kernels  41.7 us (98%)
  between operations  0.64 us (2%)
    pallas_call x1, Pallas kernels, local(): pl.pallas_call(first_kernel, out_shape=(held, held, fbuf((M, 2 * M)), fbu...  37.8 us
    pallas_call x1, Pallas kernels, local(): pl.pallas_call(last_kernel, out_shape=(full, full, small, small), in_spec...  3.91 us

profile of v1, /device:TPU:1, one launch (start us, length us, event | category | flops | bytes accessed | tf_op | source)
XLA Modules:
  0.0 42.4 jit_solution(17626448104648239725)
XLA Ops:
  0.6 37.8 %gram_and_image.1 = (f32[8,64,16,128]{3,2,1,0:T(8,128)S(1)}, f32[8,64,16,128]{3,2,1,0:T(8,128)S(1)}, f32[64,128]{1,0:T(8,128)S(1)}, f32[64,64]{1,0:T(8,128)S(1)}) custom-call(f32[64,8,16,128]{3,2,1,0:T(8,128)} %snap.1, s32[8,16,128]{2,1,0:T(8,128)} %mat_in.1), custom_call_target="tpu_custom_call" | custom-call | tf_op jit(solution)/shard_map/gram_and_image/pallas_call | solution.py:404
  38.5 3.9 %write_results.1 = (f32[64,8,16,128]{3,2,1,0:T(8,128)}, f32[64,8,16,128]{3,2,1,0:T(8,128)}, f32[64,64]{1,0:T(8,128)}, f32[64,64]{1,0:T(8,128)}) custom-call(f32[8,64,16,128]{3,2,1,0:T(8,128)S(1)} %get-tuple-element.8.basis_v, f32[8,64,16,128]{3,2,1,0:T(8,128)S(1)} %get-tuple-element.9.applied_v, f32[64,128]{1,0:T(8,128)S(1)} %get-tuple-element.10.w_in, ...), custom_call_target="tpu_custom_call" | custom-call | tf_op jit(solution)/shard_map/write_results/pallas_call | solution.py:446

commit v2 on v1

--- a/solution.py
+++ b/solution.py
@@ -41,12 +41,35 @@
     return slice(z * NY, (z + 1) * NY)
 
 
+def square_ids(rows, cols):
+    return (
+        lax.broadcasted_iota(jnp.int32, (rows, cols), 0),
+        lax.broadcasted_iota(jnp.int32, (rows, cols), 1),
+    )
+
+
 def pack(g):
-    return jnp.concatenate([g[0:32], g[32:64]], axis=1)
-
-
-def unpack(g):
-    return jnp.concatenate([g[:, 0:64], g[:, 64:128]], axis=0)
+    ri, ci = square_ids(32, M)
+    lower = jnp.concatenate([g[32:64, 32:64], g[32:64, 0:32]], axis=1)
+    both = jnp.where(ri > ci, lower, g[0:32])
+    diag = jnp.sum(jnp.where(ri + 32 == ci, g[32:64], 0.0), axis=0, keepdims=True)
+    diag = jnp.concatenate([diag, diag], axis=1)
+    return [
+        jnp.concatenate([both[k : k + 8], both[k + 8 : k + 16]], axis=1) for k in (0, 16)
+    ], diag
+
+
+def unpack(halves, diag):
+    both = jnp.concatenate([p for h in halves for p in (h[:, 0:M], h[:, M : 2 * M])], axis=0)
+    ri, ci = square_ids(32, M)
+    upper = jnp.where(ri < ci, both, 0.0)
+    lower = jnp.where(ri > ci, both, 0.0)
+    lower = jnp.concatenate([lower[:, 32:64], lower[:, 0:32]], axis=1)
+    off = jnp.concatenate([upper, lower], axis=0)
+    on = jnp.concatenate(
+        [jnp.where(ri == ci, both, 0.0), jnp.where(ri + 32 == ci, diag[:, 0:M], 0.0)], axis=0
+    )
+    return off + off.T + on
 
 
 def nt_dot(a, b):
@@ -84,8 +107,8 @@
 
 def first_kernel(
     snap, mat_in, basis_v, applied_v, w_out, pt_out,
-    mat, fld, lay, f3, i3, hz_out, hz_lo, hz_hi, cond, faces, coef, acc, acc2,
-    mine, from_c, xy_buf, z_buf, half, whole, lst,
+    mat, fld, lay, f3, i3, hz_lo, hz_hi, cond, faces, coef, acc, acc2,
+    mine, rows_buf, z_buf, half, lst,
     load_sem, fx_send, fx_recv, ar_send, ar_recv,
 ):
     r = lax.axis_index("rows")
@@ -93,7 +116,6 @@
     xy, c = r // 2, r % 2
     up_r, dn_r = (r + 1) % ROWS, (r + ROWS - 1) % ROWS
     up_z, dn_z = (z + 1) % HEIGHT, (z + HEIGHT - 1) % HEIGHT
-    partner = (xy * 2 + (1 - c), z)
 
     def remote(src, dst, ss, rs, dev):
         return pltpu.make_async_remote_copy(
@@ -115,13 +137,11 @@
     def greet(dev):
         pl.semaphore_signal(bar, inc=1, device_id=dev, device_id_type=MESH)
 
-    greet((up_r, z))
-    greet((dn_r, z))
-    greet(partner)
-    for k in range(1, 16):
-        greet((((xy + k) % 16) * 2 + c, z))
+    for k in range(1, ROWS):
+        greet(((r + k) % ROWS, z))
     for k in range(1, HEIGHT):
         greet((r, (z + k) % HEIGHT))
+        greet((xy * 2 + (1 - c), (z + k) % HEIGHT))
 
     drain(mat, load_sem.at[NXL])
     cond[...] = lookup(mat[...], CONDUCT_TABLE)
@@ -129,6 +149,29 @@
     faces[1] = cond[0]
     faces[2, 0:8] = cond[:, NZL - 1, :]
     faces[3, 0:8] = cond[:, 0, :]
+    pl.semaphore_wait(bar, ROWS - 1 + 2 * (HEIGHT - 1))
+    remote(faces.at[0], faces.at[4], fx_send.at[0], fx_recv.at[0], (up_r, z)).start()
+    remote(faces.at[1], faces.at[5], fx_send.at[1], fx_recv.at[1], (dn_r, z)).start()
+    remote(faces.at[2, 0:8], faces.at[6, 0:8], fx_send.at[2], fx_recv.at[2], (r, up_z)).start()
+    remote(faces.at[3, 0:8], faces.at[7, 0:8], fx_send.at[3], fx_recv.at[3], (r, dn_z)).start()
+
+    def face_body(x, carry):
+        remote(
+            snap.at[:, x, NZL - 1, :], hz_lo.at[x], fx_send.at[4], fx_recv.at[4], (r, up_z)
+        ).start()
+        remote(snap.at[:, x, 0, :], hz_hi.at[x], fx_send.at[5], fx_recv.at[5], (r, dn_z)).start()
+        return carry
+
+    for zz in range(NZL):
+        remote(
+            snap.at[:, 0, zz, :], lay.at[NXL + 1, :, zsl(zz)], fx_send.at[6], fx_recv.at[6],
+            (dn_r, z),
+        ).start()
+        remote(
+            snap.at[:, NXL - 1, zz, :], lay.at[0, :, zsl(zz)], fx_send.at[7], fx_recv.at[7],
+            (up_r, z),
+        ).start()
+    lax.fori_loop(0, NXL, face_body, 0)
     acc[...] = jnp.zeros_like(acc)
     acc2[...] = jnp.zeros_like(acc2)
 
@@ -136,85 +179,61 @@
         for zz in range(NZL):
             v = slab(x, zz)
             lay[x + 1, :, zsl(zz)] = v
-            if zz == 0:
-                hz_out[0, x] = v
-            if zz == NZL - 1:
-                hz_out[1, x] = v
             h, m, low = split3(v)
             f3[x, 0:64, zsl(zz)] = h
             f3[x, 64:128, zsl(zz)] = m
             f3[x, 128:192, zsl(zz)] = low
         acc[...] += nt_dot(f3[x, 0:128], f3[x])
 
-    def send_z(x):
-        remote(hz_out.at[1, x], hz_lo.at[x], fx_send.at[4], fx_recv.at[4], (r, up_z)).start()
-        remote(hz_out.at[0, x], hz_hi.at[x], fx_send.at[5], fx_recv.at[5], (r, dn_z)).start()
-
     drain(fld.at[0], load_sem.at[0])
     gram_part(0)
     drain(fld.at[NXL - 1], load_sem.at[NXL - 1])
 
-    pl.semaphore_wait(bar, 2 + 1 + 15 + 7)
-    remote(faces.at[0], faces.at[4], fx_send.at[0], fx_recv.at[0], (up_r, z)).start()
-    remote(faces.at[1], faces.at[5], fx_send.at[1], fx_recv.at[1], (dn_r, z)).start()
-    remote(faces.at[2, 0:8], faces.at[6, 0:8], fx_send.at[2], fx_recv.at[2], (r, up_z)).start()
-    remote(faces.at[3, 0:8], faces.at[7, 0:8], fx_send.at[3], fx_recv.at[3], (r, dn_z)).start()
-    remote(lay.at[1], lay.at[NXL + 1], fx_send.at[6], fx_recv.at[6], (dn_r, z)).start()
-    send_z(0)
     gram_part(NXL - 1)
-    remote(lay.at[NXL], lay.at[0], fx_send.at[7], fx_recv.at[7], (up_r, z)).start()
-    send_z(NXL - 1)
 
     def gram_body(x, carry):
         drain(fld.at[x], load_sem.at[x])
         gram_part(x)
-        send_z(x)
         return carry
 
     lax.fori_loop(1, NXL - 1, gram_body, 0)
 
-    def sum_start(i, value):
-        mine[i] = value
-        remote(
-            mine.at[i, pl.ds(pl.multiple_of((1 - c) * 16, 16), 16)], from_c.at[i],
-            ar_send.at[4 * i], ar_recv.at[4 * i], partner,
-        ).start()
-
-    def sum_xy(i):
-        drain(from_c.at[i], ar_recv.at[4 * i])
-        half[i, 0] = mine[i, pl.ds(pl.multiple_of(c * 16, 16), 16), :] + from_c[i]
-        for k in range(1, 16):
+    def sum_rows(i, value):
+        halves, diag = value
+        for h in range(2):
+            mine[i, h, 0:8] = halves[h]
+            mine[i, h, 8:9] = diag
+        for k in range(1, ROWS):
+            to = (r + k) % ROWS
             remote(
-                half.at[i, 0], xy_buf.at[i, xy], ar_send.at[4 * i + 1], ar_recv.at[4 * i + 1],
-                (((xy + k) % 16) * 2 + c, z),
+                mine.at[i, to % 2], rows_buf.at[i, r], ar_send.at[2 * i], ar_recv.at[2 * i], (to, z)
             ).start()
-        xy_buf[i, xy] = half[i, 0]
+        rows_buf[i, r] = mine[i, c]
 
     def sum_z(i):
-        drain(xy_buf.at[i, 0:15], ar_recv.at[4 * i + 1])
-        half[i, 1] = tree_sum([xy_buf[i, k] for k in range(16)])
-        for k in range(1, HEIGHT):
+        drain(rows_buf.at[i, 0 : ROWS - 1], ar_recv.at[2 * i])
+        half[i] = tree_sum([rows_buf[i, k] for k in range(ROWS)])
+        slot = c * HEIGHT + z
+        for k in range(1, 2 * HEIGHT):
+            to = (slot + k) % (2 * HEIGHT)
             remote(
-                half.at[i, 1], z_buf.at[i, z], ar_send.at[4 * i + 2], ar_recv.at[4 * i + 2],
-                (r, (z + k) % HEIGHT),
+                half.at[i], z_buf.at[i, slot], ar_send.at[2 * i + 1], ar_recv.at[2 * i + 1],
+                (xy * 2 + to // HEIGHT, to % HEIGHT),
             ).start()
-        z_buf[i, z] = half[i, 1]
-
-    def sum_c(i):
-        drain(z_buf.at[i, 0:7], ar_recv.at[4 * i + 2])
-        here = whole.at[i, pl.ds(pl.multiple_of(c * 16, 16), 16)]
-        here[...] = tree_sum([z_buf[i, k] for k in range(HEIGHT)])
-        remote(here, here, ar_send.at[4 * i + 3], ar_recv.at[4 * i + 3], partner).start()
+        z_buf[i, slot] = half[i]
 
     def sum_end(i):
-        there = whole.at[i, pl.ds(pl.multiple_of((1 - c) * 16, 16), 16)]
-        drain(there, ar_recv.at[4 * i + 3])
-        return unpack(whole[i])
+        drain(z_buf.at[i, 0 : 2 * HEIGHT - 1], ar_recv.at[2 * i + 1])
+        halves = [
+            tree_sum([z_buf[i, h * HEIGHT + k, 0:8] for k in range(HEIGHT)]) for h in range(2)
+        ]
+        diag = tree_sum([z_buf[i, k, 8:9] for k in range(HEIGHT)])
+        return unpack(halves, diag)
 
     a = acc[...]
     cross = a[0:64, 64:128] + a[0:64, 128:192]
     gram = (a[0:64, 0:64] + (cross + cross.T) + a[64:128, 64:128]) * (1.0 / CELLS)
-    sum_start(0, pack(gram))
+    sum_rows(0, pack(gram))
 
     for i in range(4):
         drain(faces.at[4 + i] if i < 2 else faces.at[4 + i, 0:8], fx_recv.at[i])
@@ -256,7 +275,6 @@
         coef[4, x] = zhi
         coef[5, x] = ly
 
-    sum_xy(0)
 
     def image(x, z0, z1, part):
         def at(xx, zz):
@@ -305,19 +323,20 @@
             acc2[...] += nt_dot(f3[x], i3[x])
             return carry
 
-        def edge_body(x, carry):
+        def edge_image(x, carry):
             images(x, 0, 1)
             images(x, NZL - 1, NZL)
-
-            def both(ref):
-                return jnp.concatenate([ref[x, :, zsl(0)], ref[x, :, zsl(NZL - 1)]], axis=1)
-
-            acc2[...] += nt_dot(both(f3), both(i3))
             return carry
 
+        def edges(ref):
+            return jnp.concatenate(
+                [ref[x, :, zsl(zz)] for x in range(1, NXL - 1) for zz in (0, NZL - 1)], axis=1
+            )
+
+        lax.fori_loop(1, NXL - 1, edge_image, 0)
+        acc2[...] += nt_dot(edges(f3), edges(i3))
+        sum_z(0)
         lax.fori_loop(0, 2, end_body, 0)
-        sum_z(0)
-        lax.fori_loop(1, NXL - 1, edge_body, 0)
 
     outer()
 
@@ -327,9 +346,7 @@
         + (a[0:64, 64:128] + a[64:128, 0:64])
         + (a[0:64, 128:192] + a[64:128, 64:128] + a[128:192, 0:64])
     ) * (1.0 / CELLS)
-    sum_start(1, pack(proj))
-    sum_xy(1)
-    sum_c(0)
+    sum_rows(1, pack(0.5 * (proj + proj.T)))
     g = sum_end(0)
 
     ri = lax.broadcasted_iota(jnp.int32, (M, M), 0)
@@ -362,7 +379,6 @@
         return carry
 
     lax.fori_loop(0, NXL, inverse_body, 0)
-    sum_c(1)
 
     for i in range(4):
         drain(faces.at[4] if i < 2 else faces.at[4, 0:8], fx_send.at[i])
@@ -371,10 +387,8 @@
     drain(lay.at[0], fx_send.at[6])
     drain(lay.at[0], fx_send.at[7])
     for i in range(2):
-        drain(from_c.at[i], ar_send.at[4 * i])
-        drain(xy_buf.at[i, 0:15], ar_send.at[4 * i + 1])
-        drain(z_buf.at[i, 0:7], ar_send.at[4 * i + 2])
-        drain(from_c.at[i], ar_send.at[4 * i + 3])
+        drain(rows_buf.at[i, 0 : ROWS - 1], ar_send.at[2 * i])
+        drain(z_buf.at[i, 0 : 2 * HEIGHT - 1], ar_send.at[2 * i + 1])
     pt_out[...] = sum_end(1)
 
 
@@ -412,7 +426,6 @@
             fbuf((NXL + 2, M, LANES)),
             wide,
             wide,
-            fbuf((2, NXL, M, NY)),
             fbuf((NXL, M, NY)),
             fbuf((NXL, M, NY)),
             fbuf((NXL, NZL, NY)),
@@ -420,18 +433,16 @@
             fbuf((6, NXL, NZL, NY)),
             fbuf((128, 192)),
             fbuf((192, 192)),
-            fbuf((2, 32, 128)),
-            fbuf((2, 16, 128)),
-            fbuf((2, 16, 16, 128)),
-            fbuf((2, 8, 16, 128)),
-            fbuf((2, 2, 16, 128)),
-            fbuf((2, 32, 128)),
+            fbuf((2, 2, 9, 128)),
+            fbuf((2, ROWS, 9, 128)),
+            fbuf((2, 2 * HEIGHT, 9, 128)),
+            fbuf((2, 9, 128)),
             pltpu.VMEM((128, 256), BF16),
             dma((NXL + 1,)),
             dma((8,)),
             dma((8,)),
-            dma((8,)),
-            dma((8,)),
+            dma((4,)),
+            dma((4,)),
         ],
         compiler_params=pltpu.CompilerParams(
             collective_id=0, has_side_effects=True, vmem_limit_bytes=32 << 20

time: 42.5 us -> 40.5 us (0.953)
  Pallas kernels: 41.7 us -> 39.7 us
    pallas_call x1, Pallas kernels: 37.8 us -> 35.8 us  [local(): pl.pallas_call(first_kernel, out_shape=(held, held, fbuf((M, 2 * M)), fbu...]
where the time goes in v2:
time: 40.5 us; the launch traced here: 40.4 us
  Pallas kernels  39.7 us (98%)
  between operations  0.64 us (2%)
    pallas_call x1, Pallas kernels, local(): pl.pallas_call(first_kernel, out_shape=(held, held, fbuf((M, 2 * M)), fbu...  35.8 us
    pallas_call x1, Pallas kernels, local(): pl.pallas_call(last_kernel, out_shape=(full, full, small, small), in_spec...  3.91 us

profile of v2, /device:TPU:1, one launch (start us, length us, event | category | flops | bytes accessed | tf_op | source)
XLA Modules:
  0.0 40.4 jit_solution(8775327723969036182)
XLA Ops:
  0.6 35.8 %gram_and_image.1 = (f32[8,64,16,128]{3,2,1,0:T(8,128)S(1)}, f32[8,64,16,128]{3,2,1,0:T(8,128)S(1)}, f32[64,128]{1,0:T(8,128)S(1)}, f32[64,64]{1,0:T(8,128)S(1)}) custom-call(f32[64,8,16,128]{3,2,1,0:T(8,128)} %snap.1, s32[8,16,128]{2,1,0:T(8,128)} %mat_in.1), custom_call_target="tpu_custom_call" | custom-call | tf_op jit(solution)/shard_map/gram_and_image/pallas_call | solution.py:418
  36.5 3.9 %write_results.1 = (f32[64,8,16,128]{3,2,1,0:T(8,128)}, f32[64,8,16,128]{3,2,1,0:T(8,128)}, f32[64,64]{1,0:T(8,128)}, f32[64,64]{1,0:T(8,128)}) custom-call(f32[8,64,16,128]{3,2,1,0:T(8,128)S(1)} %get-tuple-element.8.basis_v, f32[8,64,16,128]{3,2,1,0:T(8,128)S(1)} %get-tuple-element.9.applied_v, f32[64,128]{1,0:T(8,128)S(1)} %get-tuple-element.10.w_in, ...), custom_call_target="tpu_custom_call" | custom-call | tf_op jit(solution)/shard_map/write_results/pallas_call | solution.py:457

commit v3 on v2

--- a/solution.py
+++ b/solution.py
@@ -162,6 +162,7 @@
         remote(snap.at[:, x, 0, :], hz_hi.at[x], fx_send.at[5], fx_recv.at[5], (r, dn_z)).start()
         return carry
 
+    lax.fori_loop(0, NXL, face_body, 0)
     for zz in range(NZL):
         remote(
             snap.at[:, 0, zz, :], lay.at[NXL + 1, :, zsl(zz)], fx_send.at[6], fx_recv.at[6],
@@ -171,7 +172,6 @@
             snap.at[:, NXL - 1, zz, :], lay.at[0, :, zsl(zz)], fx_send.at[7], fx_recv.at[7],
             (up_r, z),
         ).start()
-    lax.fori_loop(0, NXL, face_body, 0)
     acc[...] = jnp.zeros_like(acc)
     acc2[...] = jnp.zeros_like(acc2)
 
@@ -314,8 +314,6 @@
     def outer():
         drain(hz_lo, fx_recv.at[4])
         drain(hz_hi, fx_recv.at[5])
-        drain(lay.at[NXL + 1], fx_recv.at[6])
-        drain(lay.at[0], fx_recv.at[7])
 
         def end_body(i, carry):
             x = i * (NXL - 1)
@@ -336,6 +334,8 @@
         lax.fori_loop(1, NXL - 1, edge_image, 0)
         acc2[...] += nt_dot(edges(f3), edges(i3))
         sum_z(0)
+        drain(lay.at[NXL + 1], fx_recv.at[6])
+        drain(lay.at[0], fx_recv.at[7])
         lax.fori_loop(0, 2, end_body, 0)
 
     outer()

time: 40.5 us -> 40.4 us (level)
  no operation moved by 1% of the time
where the time goes in v3:
time: 40.4 us; the launch traced here: 40.3 us
  Pallas kernels  39.7 us (98%)
  between operations  0.64 us (2%)
    pallas_call x1, Pallas kernels, local(): pl.pallas_call(first_kernel, out_shape=(held, held, fbuf((M, 2 * M)), fbu...  35.8 us
    pallas_call x1, Pallas kernels, local(): pl.pallas_call(last_kernel, out_shape=(full, full, small, small), in_spec...  3.91 us

profile of v3, /device:TPU:1, one launch (start us, length us, event | category | flops | bytes accessed | tf_op | source)
XLA Modules:
  0.0 40.3 jit_solution(9878106845569842903)
XLA Ops:
  0.6 35.8 %gram_and_image.1 = (f32[8,64,16,128]{3,2,1,0:T(8,128)S(1)}, f32[8,64,16,128]{3,2,1,0:T(8,128)S(1)}, f32[64,128]{1,0:T(8,128)S(1)}, f32[64,64]{1,0:T(8,128)S(1)}) custom-call(f32[64,8,16,128]{3,2,1,0:T(8,128)} %snap.1, s32[8,16,128]{2,1,0:T(8,128)} %mat_in.1), custom_call_target="tpu_custom_call" | custom-call | tf_op jit(solution)/shard_map/gram_and_image/pallas_call | solution.py:418
  36.4 3.9 %write_results.1 = (f32[64,8,16,128]{3,2,1,0:T(8,128)}, f32[64,8,16,128]{3,2,1,0:T(8,128)}, f32[64,64]{1,0:T(8,128)}, f32[64,64]{1,0:T(8,128)}) custom-call(f32[8,64,16,128]{3,2,1,0:T(8,128)S(1)} %get-tuple-element.8.basis_v, f32[8,64,16,128]{3,2,1,0:T(8,128)S(1)} %get-tuple-element.9.applied_v, f32[64,128]{1,0:T(8,128)S(1)} %get-tuple-element.10.w_in, ...), custom_call_target="tpu_custom_call" | custom-call | tf_op jit(solution)/shard_map/write_results/pallas_call | solution.py:457
